TPU v7x, 256 devices: a whole 4x4x8 slice. The times are simulated.
256 devices in a mesh: row: 16 (over z, x_hi), col: 16 (over y, x_lo, core).
Axes of the slice: x: 4 (x_hi: 2, x_lo: 2; x = x_hi * 2 + x_lo), y: 4, z: 8, core: 2. Of those that a mesh axis runs over, the one named last changes fastest.
Arguments:
- snapshot: bfloat16 [1024, 1024, 512], P('row', 'col'), may hold values from -6 to 6
- basis_two: bfloat16 [1024, 128], P('col'), may hold values from -0.1875 to 0.1875
- basis_three: bfloat16 [512, 128], replicated, may hold values from -0.25 to 0.25
Outputs:
- gram: float32 [1024, 1024], P('row', 'col')
All inputs are finite; a program needn't handle non-finite values.
Results may differ from a plain program's by a relative error of at most 0.0017.
Values may be sent and summed in bfloat16 or wider, within the bound.
A program may use at most 64 MiB of HBM per device.

v0:
```python
import jax
import jax.numpy as jnp
from jax import lax
from jax.sharding import PartitionSpec as P


def from_everyone(array, axis):
    copies = jnp.broadcast_to(array, (lax.axis_size(axis), *array.shape))
    return lax.all_to_all(copies, axis, split_axis=0, concat_axis=0, tiled=True)


def laid_out(pieces, dim):
    pieces = jnp.moveaxis(pieces, 0, dim)
    shape = pieces.shape
    return pieces.reshape(*shape[:dim], shape[dim] * shape[dim + 1], *shape[dim + 2 :])


def gather_directly(array, axis, dim):
    pieces = from_everyone(array, axis)
    return laid_out(pieces, dim)


def split_up(array, dim, size):
    before, after = (array.shape[:dim], array.shape[dim + 1 :])
    return jnp.moveaxis(array.reshape(*before, size, -1, *after), dim, 0)


def summed_on_arrival(array, axis, dim):
    size = lax.axis_size(axis)
    pieces = lax.all_to_all(split_up(array, dim, size), axis, 0, 0, tiled=True)
    return jnp.sum(pieces, axis=0)


def on_device(snapshot, basis_two, basis_three):
    cells_one, cells_two, cells_three = snapshot.shape
    ranks_two = basis_two.shape[1]
    ranks_three = basis_three.shape[1]
    inner = jnp.dot(
        snapshot.reshape(cells_one * cells_two, cells_three),
        basis_three,
        preferred_element_type=jnp.float32,
    )
    inner = inner.astype(jnp.bfloat16).reshape(cells_one, cells_two, ranks_three)
    regrouped = lax.all_to_all(inner, "col", split_axis=2, concat_axis=1, tiled=True)
    whole_factor = gather_directly(basis_two, "col", 0)
    full = jnp.einsum("abr,bq->qar", regrouped, whole_factor, preferred_element_type=jnp.float32)
    rounded = lax.all_to_all(
        full.astype(jnp.bfloat16), "col", split_axis=0, concat_axis=2, tiled=True
    )
    partial_gram = jnp.einsum(
        "qar,qbr->ab",
        rounded,
        gather_directly(rounded, "row", 1),
        preferred_element_type=jnp.float32,
    )
    summed_gram = summed_on_arrival(partial_gram, "col", 1)
    return summed_gram * (1.0 / (ranks_two * ranks_three))


def solution(mesh):
    in_specs = (P("row", "col", None), P("col", None), P())
    out_specs = P("row", "col")
    return jax.shard_map(
        on_device, mesh=mesh, in_specs=in_specs, out_specs=out_specs, check_vma=False
    )
```

profile of v0, /device:TPU:1, one launch (start us, length us, event | category | flops | bytes accessed | tf_op | source)
XLA Modules:
  0.0 133.6 jit_solution(17687879233535887853)
XLA Ops:
  0.0 0.0 copy-start
  0.0 0.9 copy-done
  0.9 3.4 %convolution_convert_fusion = bf16[4096,128]{1,0:T(8,128)(2,1)S(1)} fusion(bf16[4096,512]{1,0:T(8,128)(2,1)} %bitcast.59, bf16[512,128]{1,0:T(8,128)(2,1)S(1)} %copy-done), kind=kOutput, calls=%fused_computation | convolution fusion | flops 537395200 | bytes 5373952 | tf_op jit(solution)/shard_map/dot_general | solution.py:38
  4.4 3.0 %copy.23 = bf16[64,64,128]{1,0,2:T(8,128)(2,1)S(1)} copy(bf16[64,64,128]{2,1,0:T(8,128)(2,1)S(1)} %bitcast.60) | data formatting | bytes 2097152 | tf_op jit(solution)/shard_map/reshape | solution.py:43
  7.3 0.0 copy-start.1
  7.4 1.5 %reshape.19 = bf16[16,2,16384]{2,1,0:T(2,128)(2,1)S(1)} reshape(bf16[128,64,64]{2,1,0:T(8,128)(2,1)S(1)} %bitcast.58) | data formatting | bytes 2097152
  8.8 22.1 %all_to_all.48 = bf16[16,2,16384]{2,1,0:T(2,128)(2,1)S(1)} all-to-all(bf16[16,2,16384]{2,1,0:T(2,128)(2,1)S(1)} %reshape.19), channel_id=1, replica_groups=mesh['row'=16,'col'=16] {'col'}, dimensions={0} | all-to-all | bytes 2097152 | tf_op jit(solution)/shard_map/all_to_all | solution.py:44
  30.9 0.0 copy-done.1
  30.9 0.7 broadcast_in_dim.6
  31.7 4.5 %all-to-all-start.1 = ((bf16[16,64,128]{2,1,0:T(8,128)(2,1)}), bf16[16,64,128]{2,1,0:T(8,128)(2,1)S(1)}, u32[]{:S(2)}, u32[]{:S(2)}) async-start(bf16[16,64,128]{2,1,0:T(8,128)(2,1)} %broadcast_in_dim.6), calls=%async_computation.1 | async-start | bytes 524288 | tf_op jit(solution)/shard_map/all_to_all | solution.py:9
  36.2 1.3 reshape.20
  37.5 5.9 %all-to-all-done.1 = bf16[16,64,128]{2,1,0:T(8,128)(2,1)S(1)} async-done(((bf16[16,64,128]{2,1,0:T(8,128)(2,1)}), bf16[16,64,128]{2,1,0:T(8,128)(2,1)S(1)}, u32[]{:S(2)}, u32[]{:S(2)}) %all-to-all-start.1) | async-done | bytes 262176 | tf_op jit(solution)/shard_map/all_to_all | solution.py:9
  43.4 1.4 %fusion.14 = bf16[128,64,8]{0,2,1:T(8,128)(2,1)S(1)} fusion(bf16[64,64,128]{1,0,2:T(8,128)(2,1)S(1)} %bitcast.63, bf16[16,64,128]{2,1,0:T(8,128)(2,1)S(1)} %all-to-all-done.1), kind=kOutput, calls=%fused_computation.9 | convolution fusion | flops 134283264 | bytes 1441792 | tf_op jit(solution)/shard_map/abr,bq->qar/dot_general | solution.py:46
  44.8 0.2 copy.25
  45.0 0.2 reshape.21
  45.3 9.6 %all_to_all.49 = bf16[16,2,2048]{2,1,0:T(2,128)(2,1)S(1)} all-to-all(bf16[16,2,2048]{2,1,0:T(2,128)(2,1)S(1)} %reshape.21), channel_id=1, replica_groups=mesh['row'=16,'col'=16] {'col'}, dimensions={0} | all-to-all | bytes 262144 | tf_op jit(solution)/shard_map/all_to_all | solution.py:47
  54.9 0.2 reshape.22
  55.2 0.1 copy.27
  55.3 0.5 broadcast_in_dim.7
  55.9 61.1 %all_to_all.50 = bf16[16,8,64,128]{3,2,1,0:T(8,128)(2,1)S(1)} all-to-all(bf16[16,8,64,128]{3,2,1,0:T(8,128)(2,1)S(1)} %broadcast_in_dim.7), channel_id=1, replica_groups=mesh['row'=16,'col'=16] {'row'}, dimensions={0} | all-to-all | bytes 4194304 | tf_op jit(solution)/shard_map/all_to_all | solution.py:9
  116.9 1.1 fusion.5
  118.1 0.3 reshape.23
  118.4 12.5 %all_to_all.51 = f32[16,1,4096]{2,1,0:T(1,128)S(1)} all-to-all(f32[16,1,4096]{2,1,0:T(1,128)S(1)} %reshape.23), channel_id=1, replica_groups=mesh['row'=16,'col'=16] {'col'}, dimensions={0} | all-to-all | bytes 524288 | tf_op jit(solution)/shard_map/all_to_all | solution.py:30
  130.9 0.5 broadcast
  131.4 1.3 reduce
  132.7 0.2 reshape.24
  132.9 0.6 broadcast_multiply_fusion
  (2 shorter events, 0.1 us)
Async XLA Ops:
  0.0 0.9 copy-start
  7.3 23.6 %copy-start.1 = (bf16[64,128]{1,0:T(8,128)(2,1)S(1)}, bf16[64,128]{1,0:T(8,128)(2,1)}, u32[]{:S(2)}) copy-start(bf16[64,128]{1,0:T(8,128)(2,1)} %param.4) | copy-start | bytes 49156
  31.7 11.7 %all-to-all-start.1 = ((bf16[16,64,128]{2,1,0:T(8,128)(2,1)}), bf16[16,64,128]{2,1,0:T(8,128)(2,1)S(1)}, u32[]{:S(2)}, u32[]{:S(2)}) async-start(bf16[16,64,128]{2,1,0:T(8,128)(2,1)} %broadcast_in_dim.6), calls=%async_computation.1 | async-start | bytes 524288 | tf_op jit(solution)/shard_map/all_to_all | solution.py:9
where the time goes:
time: 134 us
  blocking collectives  105 us (78%)
  local copies, waits for them, and re-layouts  9.85 us (7%)
  matrix products  6 us (4%)
  waiting for transfers between devices  5.89 us (4%)
  starting transfers between devices  4.49 us (3%)
  other arithmetic  1.93 us (1%)
    all_to_all x1, blocking collectives, from_everyone(): return lax.all_to_all(copies, axis, split_axis=0, concat_axis=0, tiled=True)  61.1 us
    all_to_all x1, blocking collectives, on_device(): lax.all_to_all(inner, 'col', split_axis=2, concat_axis=1, tiled=True)  22.1 us
    all_to_all x1, blocking collectives, summed_on_arrival(): pieces = lax.all_to_all(split_up(array, dim, size), axis, 0, 0, tiled=True)  12.5 us
    all_to_all x1, blocking collectives, on_device(): lax.all_to_all(full.astype(jnp.bfloat16), 'col', split_axis=0, concat_axi...  9.64 us
    all_to_all x1, waiting for transfers between devices, from_everyone(): return lax.all_to_all(copies, axis, split_axis=0, concat_axis=0, tiled=True)  5.89 us
    unnamed x10, local copies, waits for them, and re-layouts  4.69 us
    all_to_all x1, starting transfers between devices, from_everyone(): return lax.all_to_all(copies, axis, split_axis=0, concat_axis=0, tiled=True)  4.49 us
    dot_general x1, matrix products, on_device(): jnp.dot(snapshot.reshape(cells_one * cells_two, cells_three), basis_three...  3.44 us
  transfers between devices with their start and end apart: 1, of which 1 were waited for; matrix products, arithmetic and copies ran while one was open for 1% of the time, Pallas kernels for 0%

commit v1 on v0

v1 whole, which is shorter than its diff:
```python
import jax
import jax.numpy as jnp
from jax import lax
from jax.experimental import pallas as pl
from jax.experimental.pallas import tpu as pltpu
from jax.sharding import PartitionSpec as P

MESH = pl.DeviceIdType.MESH
NT = (((1,), (1,)), ((), ()))

N_COL = 16
PLANES = 8
STAGES = 4
OFFSETS = (0, -2, -1, 2)
BLOCKS = ((0, 0), (0, 2), (2, 0), (0, 3), (3, 0), (2, 3), (3, 2), (1, 3))


def kernel(
    snap_hbm,
    b2_ref,
    b3_ref,
    out_ref,
    snap,
    b3t,
    factor,
    weights,
    outgoing,
    incoming,
    pacc,
    half_out,
    rows,
    grams,
    parts,
    load_sems,
    factor_sems,
    a_send,
    a_recv,
    x_send,
    x_recv,
    z_send,
    z_recv,
    g_send,
    g_recv,
):
    row = lax.axis_index("row")
    col = lax.axis_index("col")
    z = row // 2
    xh = lax.rem(row, 2)
    core = lax.rem(col, 2)

    def plane(offset):
        return lax.rem(z + offset + PLANES, PLANES)

    loads = [
        pltpu.make_async_copy(snap_hbm.at[pl.ds(16 * s, 16)], snap.at[s], load_sems.at[s])
        for s in range(STAGES)
    ]
    for load in loads:
        load.start()

    barrier = pltpu.get_barrier_semaphore()

    def greet(i, carry):
        peer = lax.rem(col + i, N_COL)
        pl.semaphore_signal(barrier, inc=1, device_id=(row, peer), device_id_type=MESH)
        return carry

    lax.fori_loop(1, N_COL, greet, 0)
    pl.semaphore_signal(barrier, inc=1, device_id=(z * 2 + 1 - xh, col), device_id_type=MESH)
    for offset in OFFSETS[1:]:
        pl.semaphore_signal(barrier, inc=1, device_id=(plane(offset) * 2 + xh, col), device_id_type=MESH)

    b3t[...] = b3_ref[...].T

    def first_product(s):
        loads[s].wait()
        left = b3t[...]
        for jp in range(4):
            right = jnp.concatenate(
                [snap[s, 2 * jp], snap[s, 8 + 2 * jp], snap[s, 2 * jp + 1], snap[s, 9 + 2 * jp]], axis=0
            )
            inner = lax.dot_general(left, right, NT, preferred_element_type=jnp.float32)
            pair = jnp.concatenate(
                [inner[:, :128].reshape(N_COL, 8, 128), inner[:, 128:].reshape(N_COL, 8, 128)], axis=1
            ).astype(jnp.bfloat16)
            outgoing[s, :, jp] = pair
        incoming[s, col] = outgoing[s, col]

    def send_stage(s):
        def body(i, carry):
            peer = col ^ i
            pltpu.make_async_remote_copy(
                src_ref=outgoing.at[s, peer],
                dst_ref=incoming.at[s, col],
                send_sem=a_send.at[s],
                recv_sem=a_recv.at[s],
                device_id=(row, peer),
                device_id_type=MESH,
            ).start()
            return carry

        lax.fori_loop(1, N_COL, body, 0)

    def stage_copy(s):
        return pltpu.make_async_remote_copy(
            src_ref=outgoing.at[s, pl.ds(0, N_COL - 1)],
            dst_ref=incoming.at[s, pl.ds(0, N_COL - 1)],
            send_sem=a_send.at[s],
            recv_sem=a_recv.at[s],
            device_id=(row, col),
            device_id_type=MESH,
        )

    first_product(0)
    pl.semaphore_wait(barrier, N_COL - 1 + 1 + 3)

    def send_factor(i, carry):
        peer = col ^ i
        pltpu.make_async_remote_copy(
            src_ref=b2_ref,
            dst_ref=factor.at[col],
            send_sem=factor_sems.at[0],
            recv_sem=factor_sems.at[1],
            device_id=(row, peer),
            device_id_type=MESH,
        ).start()
        return carry

    lax.fori_loop(1, N_COL, send_factor, 0)
    send_stage(0)
    factor[col] = b2_ref[...]
    for s in range(1, STAGES):
        first_product(s)
        send_stage(s)

    factor_copy = pltpu.make_async_remote_copy(
        src_ref=factor.at[pl.ds(0, N_COL - 1)],
        dst_ref=factor.at[pl.ds(0, N_COL - 1)],
        send_sem=factor_sems.at[0],
        recv_sem=factor_sems.at[1],
        device_id=(row, col),
        device_id_type=MESH,
    )
    factor_copy.wait_recv()
    weights[...] = jnp.zeros_like(weights)
    for c in range(N_COL):
        block = factor[c]
        weights[pl.ds(c * 128, 64), :128] = block
        weights[pl.ds(c * 128 + 64, 64), 128:] = block

    def x_copy(s):
        return pltpu.make_async_remote_copy(
            src_ref=half_out.at[s],
            dst_ref=rows.at[0, xh, s],
            send_sem=x_send.at[s],
            recv_sem=x_recv.at[s],
            device_id=(z * 2 + 1 - xh, col),
            device_id_type=MESH,
        )

    def send_rows(s, side):
        for slot in range(1, len(OFFSETS)):
            pltpu.make_async_remote_copy(
                src_ref=rows.at[0, side, s],
                dst_ref=rows.at[slot, side, s],
                send_sem=z_send,
                recv_sem=z_recv,
                device_id=(plane(-OFFSETS[slot]) * 2 + xh, col),
                device_id_type=MESH,
            ).start()

    def second_product(s):
        stage_copy(s).wait_recv()
        total = jnp.zeros((64, 256), jnp.float32)
        for c in range(0, N_COL, 2):
            left = jnp.concatenate(
                [incoming[s, c].reshape(64, 128), incoming[s, c + 1].reshape(64, 128)], axis=1
            )
            total = total + jnp.dot(left, weights[pl.ds(c * 128, 256), :], preferred_element_type=jnp.float32)
        pacc[0] = total[:, :128]
        pacc[1] = total[:, 128:]
        for r in range(4):
            halves = []
            for h in range(2):
                every = pl.ds(4 * h + r, 8, stride=8)
                halves.append(jnp.concatenate([pacc[0, every, :], pacc[1, every, :]], axis=0))
            lanes = pl.ds(r * 128, 128)
            rows[0, xh, s, :, lanes] = jnp.where(xh == 0, halves[0], halves[1]).astype(jnp.bfloat16)
            half_out[s, :, lanes] = jnp.where(xh == 0, halves[1], halves[0]).astype(jnp.bfloat16)

    for s in range(STAGES):
        second_product(s)
        x_copy(s).start()
        send_rows(s, xh)
        if s > 0:
            x_copy(s - 1).wait_recv()
            send_rows(s - 1, 1 - xh)
    x_copy(STAGES - 1).wait_recv()
    send_rows(STAGES - 1, 1 - xh)

    z_copy = pltpu.make_async_remote_copy(
        src_ref=rows.at[pl.ds(1, 3)],
        dst_ref=rows.at[pl.ds(1, 3)],
        send_sem=z_send,
        recv_sem=z_recv,
        device_id=(row, col),
        device_id_type=MESH,
    )
    z_copy.wait_recv()

    me = xh * N_COL + col
    low = lax.broadcasted_iota(jnp.int32, (64, 128), 1) < 64

    def gram_target(b, i):
        slot_u, slot_v = BLOCKS[b]
        to_row = plane(OFFSETS[slot_u]) * 2 + i // 2
        to_col = plane(OFFSETS[slot_v]) * 2 + lax.rem(i, 2)
        return to_row, to_col

    for b, (slot_u, slot_v) in enumerate(BLOCKS):
        upper = rows[slot_u, :, 0:2].reshape(64, 512)
        lower = rows[slot_u, :, 2:4].reshape(64, 512)
        right = rows[slot_v].reshape(128, 512)
        swapped = jnp.concatenate([rows[slot_v, 1].reshape(64, 512), rows[slot_v, 0].reshape(64, 512)], axis=0)
        m1 = lax.dot_general(upper, right, NT, preferred_element_type=jnp.float32)
        m2 = lax.dot_general(lower, swapped, NT, preferred_element_type=jnp.float32)
        for_core0 = jnp.where(low, m1, m2).reshape(2, 32, 128)
        for_core1 = jnp.where(low, m2, m1).reshape(2, 32, 128)
        for xu in range(2):
            grams[b, 2 * xu] = for_core0[xu]
            grams[b, 2 * xu + 1] = for_core1[xu]

        def send_gram(i, carry):
            to_row, to_col = gram_target(b, i)
            own = jnp.logical_and(to_row == row, to_col == col)

            @pl.when(own)
            def _():
                pltpu.make_async_copy(grams.at[b, i], parts.at[me], g_recv).start()

            @pl.when(jnp.logical_not(own))
            def _():
                pltpu.make_async_remote_copy(
                    src_ref=grams.at[b, i],
                    dst_ref=parts.at[me],
                    send_sem=g_send.at[b],
                    recv_sem=g_recv,
                    device_id=(to_row, to_col),
                    device_id_type=MESH,
                ).start()

            return carry

        lax.fori_loop(0, 4, send_gram, 0)

    pltpu.make_async_copy(parts, parts, g_recv).wait()
    total = jnp.sum(parts[...], axis=0) * (1.0 / 16384.0)
    first, second = total[:, :64], total[:, 64:]
    out_ref[0:32, :] = jnp.where(core == 0, first, second)
    out_ref[32:64, :] = jnp.where(core == 0, second, first)

    factor_copy.wait_send()
    for s in range(STAGES):
        stage_copy(s).wait_send()
        x_copy(s).wait_send()
    z_copy.wait_send()
    for b in range(len(BLOCKS)):

        def end_gram(i, carry):
            to_row, to_col = gram_target(b, i)

            @pl.when(jnp.logical_not(jnp.logical_and(to_row == row, to_col == col)))
            def _():
                pltpu.make_async_remote_copy(
                    src_ref=grams.at[b, i],
                    dst_ref=parts.at[me],
                    send_sem=g_send.at[b],
                    recv_sem=g_recv,
                    device_id=(to_row, to_col),
                    device_id_type=MESH,
                ).wait_send()

            return carry

        lax.fori_loop(0, 4, end_gram, 0)


def on_device(snapshot, basis_two, basis_three):
    vmem = pl.BlockSpec(memory_space=pltpu.VMEM)
    bf16, f32 = jnp.bfloat16, jnp.float32
    dma = pltpu.SemaphoreType.DMA
    return pl.pallas_call(
        kernel,
        out_shape=jax.ShapeDtypeStruct((64, 64), f32),
        in_specs=[pl.BlockSpec(memory_space=pltpu.HBM), vmem, vmem],
        out_specs=vmem,
        scratch_shapes=[
            pltpu.VMEM((STAGES, 16, 64, 512), bf16),
            pltpu.VMEM((128, 512), bf16),
            pltpu.VMEM((N_COL, 64, 128), bf16),
            pltpu.VMEM((N_COL * 128, 256), bf16),
            pltpu.VMEM((STAGES, N_COL, 4, 16, 128), bf16),
            pltpu.VMEM((STAGES, N_COL, 4, 16, 128), bf16),
            pltpu.VMEM((2, 64, 128), f32),
            pltpu.VMEM((STAGES, 16, 512), bf16),
            pltpu.VMEM((4, 2, STAGES, 16, 512), bf16),
            pltpu.VMEM((len(BLOCKS), 4, 32, 128), f32),
            pltpu.VMEM((2 * N_COL, 32, 128), f32),
            dma((STAGES,)),
            dma((2,)),
            dma((STAGES,)),
            dma((STAGES,)),
            dma((STAGES,)),
            dma((STAGES,)),
            dma,
            dma,
            dma((len(BLOCKS),)),
            dma,
        ],
        compiler_params=pltpu.CompilerParams(
            collective_id=0, has_side_effects=True, vmem_limit_bytes=48 * 1024 * 1024
        ),
    )(snapshot, basis_two, basis_three)


def solution(mesh):
    in_specs = (P("row", "col", None), P("col", None), P())
    return jax.shard_map(
        on_device, mesh=mesh, in_specs=in_specs, out_specs=P("row", "col"), check_vma=False
    )
```

time: 134 us -> 49.3 us (0.37)
  blocking collectives: 105 us -> 0 us
  Pallas kernels: 0 us -> 44.5 us
  matrix products: 6 us -> 0 us
  waiting for transfers between devices: 5.89 us -> 0 us
  local copies, waits for them, and re-layouts: 9.85 us -> 4.43 us
  starting transfers between devices: 4.49 us -> 0 us
  other arithmetic: 1.93 us -> 0 us
    all_to_all x4 -> x0, blocking collectives: 105 us -> none  [the longest x1 61.1 us: from_everyone(): return lax.all_to_all(copies, axis, split_axis=0, concat_axis=0, tiled=True)]
    pallas_call x0 -> x1, Pallas kernels: none -> 44.5 us  [on_device(): pl.pallas_call(kernel, out_shape=jax.ShapeDtypeStruct((64, 64), f32), in_...]
    dot_general x3 -> x0, matrix products: 6 us -> none  [the longest x1 3.44 us: on_device(): jnp.dot(snapshot.reshape(cells_one * cells_two, cells_three), basis_three...]
    all_to_all x1 -> x0, waiting for transfers between devices: 5.89 us -> none  [from_everyone(): return lax.all_to_all(copies, axis, split_axis=0, concat_axis=0, tiled=True)]
    all_to_all x1 -> x0, starting transfers between devices: 4.49 us -> none  [from_everyone(): return lax.all_to_all(copies, axis, split_axis=0, concat_axis=0, tiled=True)]
    reshape x1 -> x0, local copies, waits for them, and re-layouts: 2.99 us -> none  [on_device(): inner.astype(jnp.bfloat16).reshape(cells_one, cells_two, ranks_three)]
    unnamed x10 -> x7, local copies, waits for them, and re-layouts: 4.69 us -> 4.43 us
  transfers between devices with their start and end apart: 1 -> 0, of which waited for: 1 -> 0; matrix products, arithmetic and copies ran while one was open for 1% -> 0% of each run, Pallas kernels for 0% -> 0%
where the time goes in v1:
time: 49.3 us; the launch traced here: 49 us
  Pallas kernels  44.5 us (90%)
  local copies, waits for them, and re-layouts  4.43 us (9%)
    pallas_call x1, Pallas kernels, on_device(): pl.pallas_call(kernel, out_shape=jax.ShapeDtypeStruct((64, 64), f32), in_...  44.5 us
    unnamed x7, local copies, waits for them, and re-layouts  4.43 us

profile of v1, /device:TPU:1, one launch (start us, length us, event | category | flops | bytes accessed | tf_op | source)
XLA Modules:
  0.0 49.0 jit_solution(3541125659106233207)
XLA Ops:
  0.0 0.0 copy-start
  0.0 2.2 %copy-done = bf16[64,64,512]{2,1,0:T(8,128)(2,1)S(1)} copy-done((bf16[64,64,512]{2,1,0:T(8,128)(2,1)S(1)}, bf16[64,64,512]{2,1,0:T(8,128)(2,1)}, u32[]{:S(2)}) %copy-start) | copy-done | bytes 4194328
  2.2 0.0 copy-start.1
  2.2 0.9 %copy-done.1 = bf16[512,128]{1,0:T(8,128)(2,1)S(1)} copy-done((bf16[512,128]{1,0:T(8,128)(2,1)S(1)}, bf16[512,128]{1,0:T(8,128)(2,1)}, u32[]{:S(2)}) %copy-start.1) | copy-done | bytes 131096
  3.1 0.0 copy-start.2
  3.1 0.7 %copy-done.2 = bf16[64,128]{1,0:T(8,128)(2,1)S(1)} copy-done((bf16[64,128]{1,0:T(8,128)(2,1)S(1)}, bf16[64,128]{1,0:T(8,128)(2,1)}, u32[]{:S(2)}) %copy-start.2) | copy-done | bytes 16408
  3.8 44.5 %shard_map.37 = f32[64,64]{1,0:T(8,128)S(1)} custom-call(bf16[64,64,512]{2,1,0:T(8,128)(2,1)S(1)} %copy-done, bf16[64,128]{1,0:T(8,128)(2,1)S(1)} %copy-done.2, bf16[512,128]{1,0:T(8,128)(2,1)S(1)} %copy-done.1), custom_call_target="tpu_custom_call" | custom-call | tf_op jit(solution)/shard_map/pallas_call | solution.py:292
  48.4 0.6 %copy.5 = f32[64,64]{1,0:T(8,128)} copy(f32[64,64]{1,0:T(8,128)S(1)} %shard_map.37) | data formatting | bytes 32768
Async XLA Ops:
  0.0 2.2 %copy-start = (bf16[64,64,512]{2,1,0:T(8,128)(2,1)S(1)}, bf16[64,64,512]{2,1,0:T(8,128)(2,1)}, u32[]{:S(2)}) copy-start(bf16[64,64,512]{2,1,0:T(8,128)(2,1)} %snap_hbm.1) | copy-start | bytes 12582916
  2.2 0.9 %copy-start.1 = (bf16[512,128]{1,0:T(8,128)(2,1)S(1)}, bf16[512,128]{1,0:T(8,128)(2,1)}, u32[]{:S(2)}) copy-start(bf16[512,128]{1,0:T(8,128)(2,1)} %b3_ref.1) | copy-start | bytes 393220
  3.1 0.7 %copy-start.2 = (bf16[64,128]{1,0:T(8,128)(2,1)S(1)}, bf16[64,128]{1,0:T(8,128)(2,1)}, u32[]{:S(2)}) copy-start(bf16[64,128]{1,0:T(8,128)(2,1)} %b2_ref.1) | copy-start | bytes 49156

commit v2 on v1

v2 whole, which is shorter than its diff:
```python
import jax
import jax.numpy as jnp
from jax import lax
from jax.experimental import pallas as pl
from jax.experimental.pallas import tpu as pltpu
from jax.sharding import PartitionSpec as P

MESH = pl.DeviceIdType.MESH
NT = (((1,), (1,)), ((), ()))

N_COL = 16
PLANES = 8
STAGES = 4
OFFSETS = (0, -2, -1, 2)
BLOCKS = ((3, 0), (3, 2), (1, 3), (2, 0), (2, 3), (0, 3), (0, 2), (0, 0))


def kernel(
    snap_hbm,
    b2_hbm,
    b3_hbm,
    out_ref,
    snap,
    b3,
    b3t,
    factor,
    weights,
    outgoing,
    incoming,
    pacc,
    half_out,
    rows,
    grams,
    mates,
    sums,
    parts,
    load_sems,
    f_sems,
    a_send,
    a_recv,
    z_send,
    z_recv,
    m_send,
    m_recv,
    g_send,
    g_recv,
):
    row = lax.axis_index("row")
    col = lax.axis_index("col")
    z = row // 2
    xh = lax.rem(row, 2)
    core = lax.rem(col, 2)
    chip = col // 2
    across = (1 - xh, col ^ 2)

    def plane(offset):
        return lax.rem(z + offset + PLANES, PLANES)

    def remote(src, dst, send_sem, recv_sem, device):
        return pltpu.make_async_remote_copy(
            src_ref=src,
            dst_ref=dst,
            send_sem=send_sem,
            recv_sem=recv_sem,
            device_id=device,
            device_id_type=MESH,
        )

    here = (row, col)
    load_b3 = pltpu.make_async_copy(b3_hbm, b3, load_sems.at[STAGES])
    load_b2 = pltpu.make_async_copy(b2_hbm, factor.at[core, chip], load_sems.at[STAGES + 1])
    loads = [
        pltpu.make_async_copy(snap_hbm.at[pl.ds(16 * s, 16)], snap.at[s], load_sems.at[s])
        for s in range(STAGES)
    ]
    load_b3.start()
    loads[0].start()
    load_b2.start()
    for load in loads[1:]:
        load.start()

    barrier = pltpu.get_barrier_semaphore()

    def greet(device):
        pl.semaphore_signal(barrier, inc=1, device_id=device, device_id_type=MESH)

    def greet_column(i, carry):
        greet((row, col ^ i))
        return carry

    lax.fori_loop(1, N_COL, greet_column, 0)
    for offset in OFFSETS[1:]:
        greet((plane(offset) * 2 + xh, col))
    for offset in OFFSETS:
        greet((plane(offset) * 2 + across[0], across[1]))
    for y in range(1, 4):
        greet((z * 2 + across[0], across[1] ^ (4 * y)))

    load_b3.wait()
    b3t[...] = b3[...].T

    def first_product(s):
        loads[s].wait()
        left = b3t[...]
        for jp in range(4):
            right = jnp.concatenate(
                [snap[s, 2 * jp], snap[s, 8 + 2 * jp], snap[s, 2 * jp + 1], snap[s, 9 + 2 * jp]], axis=0
            )
            inner = lax.dot_general(left, right, NT, preferred_element_type=jnp.float32)
            pair = jnp.concatenate(
                [inner[:, :128].reshape(N_COL, 8, 128), inner[:, 128:].reshape(N_COL, 8, 128)], axis=1
            ).astype(jnp.bfloat16)
            outgoing[s, :, jp] = pair
        incoming[s, col] = outgoing[s, col ^ (2 * xh)]

    def send_stage(s):
        def body(i, carry):
            peer = col ^ i
            remote(
                outgoing.at[s, peer ^ (2 * xh)], incoming.at[s, col], a_send.at[s], a_recv.at[s], (row, peer)
            ).start()
            return carry

        lax.fori_loop(1, N_COL, body, 0)

    def stage_copy(s):
        most = pl.ds(0, N_COL - 1)
        return remote(outgoing.at[s, most], incoming.at[s, most], a_send.at[s], a_recv.at[s], here)

    first_product(0)
    load_b2.wait()
    pl.semaphore_wait(barrier, N_COL - 1 + 3 + 4 + 3)

    send_stage(0)
    own = factor.at[core, chip]
    for y in range(1, 4):
        remote(own, own, f_sems.at[0], f_sems.at[1], (row, col ^ (4 * y))).start()
    for y in range(4):
        remote(own, own, f_sems.at[0], f_sems.at[1], (z * 2 + across[0], across[1] ^ (4 * y))).start()
    for s in range(1, STAGES):
        first_product(s)
        send_stage(s)

    most = factor.at[core, pl.ds(0, 7)]
    factor_copy = remote(most, most, f_sems.at[0], f_sems.at[1], here)
    factor_copy.wait_recv()
    mate = (row, col ^ 1)
    mine = factor.at[core]
    mate_copy = remote(mine, mine, f_sems.at[2], f_sems.at[3], mate)
    mate_copy.start()
    weights[...] = jnp.zeros_like(weights)
    mate_copy.wait_recv()
    for c in range(N_COL):
        block = factor[c % 2, c // 2]
        weights[pl.ds(c * 128, 64), :128] = block
        weights[pl.ds(c * 128 + 64, 64), 128:] = block

    def send_rows(s):
        for slot, offset in enumerate(OFFSETS):
            to = plane(-offset) * 2
            if slot:
                remote(rows.at[0, xh, s], rows.at[slot, xh, s], z_send.at[0], z_recv.at[0], (to + xh, col)).start()
            which = 0 if slot else 1
            remote(
                half_out.at[s],
                rows.at[slot, xh, s],
                z_send.at[which],
                z_recv.at[which],
                (to + across[0], across[1]),
            ).start()

    def second_product(s):
        stage_copy(s).wait_recv()
        total = jnp.zeros((64, 256), jnp.float32)
        for c in range(0, N_COL, 2):
            left = jnp.concatenate(
                [incoming[s, c].reshape(64, 128), incoming[s, c + 1].reshape(64, 128)], axis=1
            )
            total = total + jnp.dot(left, weights[pl.ds(c * 128, 256), :], preferred_element_type=jnp.float32)
        pacc[0] = total[:, :128]
        pacc[1] = total[:, 128:]
        for r in range(4):
            halves = []
            for h in range(2):
                every = pl.ds(4 * h + r, 8, stride=8)
                halves.append(jnp.concatenate([pacc[0, every, :], pacc[1, every, :]], axis=0))
            lanes = pl.ds(r * 128, 128)
            rows[0, xh, s, :, lanes] = jnp.where(xh == 0, halves[0], halves[1]).astype(jnp.bfloat16)
            half_out[s, :, lanes] = jnp.where(xh == 0, halves[1], halves[0]).astype(jnp.bfloat16)

    for s in range(STAGES):
        second_product(s)
        send_rows(s)

    far = rows.at[pl.ds(1, 3)]
    near = rows.at[0, 0]
    far_copy = remote(far, far, z_send.at[0], z_recv.at[0], here)
    near_copy = remote(near, near, z_send.at[1], z_recv.at[1], here)
    near_copy.wait_recv()
    far_copy.wait_recv()

    low = lax.broadcasted_iota(jnp.int32, (64, 128), 1) < 64
    sender = xh * 8 + chip

    def mate_gram(b):
        return remote(grams.at[b, 1 - core], mates.at[b], m_send.at[b], m_recv.at[b], mate)

    def gram_copy(b, j):
        slot_u, slot_v = BLOCKS[b]
        to = (plane(OFFSETS[slot_u]) * 2 + core, plane(OFFSETS[slot_v]) * 2 + j)
        own = jnp.logical_and(to[0] == row, to[1] == col)
        return own, remote(sums.at[b, j], parts.at[sender], g_send.at[b], g_recv, to)

    def send_gram(b):
        mate_gram(b).wait_recv()
        sums[b] = grams[b, core] + mates[b]
        for j in range(2):
            own, copy = gram_copy(b, j)

            @pl.when(own)
            def _():
                pltpu.make_async_copy(sums.at[b, j], parts.at[sender], g_recv).start()

            @pl.when(jnp.logical_not(own))
            def _():
                copy.start()

    for b, (slot_u, slot_v) in enumerate(BLOCKS):
        upper = rows[slot_u, :, 0:2].reshape(64, 512)
        lower = rows[slot_u, :, 2:4].reshape(64, 512)
        right = rows[slot_v].reshape(128, 512)
        swapped = jnp.concatenate([rows[slot_v, 1].reshape(64, 512), rows[slot_v, 0].reshape(64, 512)], axis=0)
        m1 = lax.dot_general(upper, right, NT, preferred_element_type=jnp.float32)
        m2 = lax.dot_general(lower, swapped, NT, preferred_element_type=jnp.float32)
        grams[b, :, 0] = jnp.where(low, m1, m2).reshape(2, 32, 128)
        grams[b, :, 1] = jnp.where(low, m2, m1).reshape(2, 32, 128)
        mate_gram(b).start()
        if b:
            send_gram(b - 1)
    send_gram(len(BLOCKS) - 1)

    pltpu.make_async_copy(parts, parts, g_recv).wait()
    total = jnp.sum(parts[...], axis=0) * (1.0 / 16384.0)
    first, second = total[:, :64], total[:, 64:]
    out_ref[0:32, :] = jnp.where(core == 0, first, second)
    out_ref[32:64, :] = jnp.where(core == 0, second, first)

    factor_copy.wait_send()
    mate_copy.wait_send()
    for s in range(STAGES):
        stage_copy(s).wait_send()
    far_copy.wait_send()
    near_copy.wait_send()
    for b in range(len(BLOCKS)):
        mate_gram(b).wait_send()
        for j in range(2):
            own, copy = gram_copy(b, j)

            @pl.when(jnp.logical_not(own))
            def _():
                copy.wait_send()


def on_device(snapshot, basis_two, basis_three):
    anywhere = pl.BlockSpec(memory_space=pl.ANY)
    bf16, f32 = jnp.bfloat16, jnp.float32
    dma = pltpu.SemaphoreType.DMA
    n_blocks = len(BLOCKS)
    return pl.pallas_call(
        kernel,
        out_shape=jax.ShapeDtypeStruct((64, 64), f32),
        in_specs=[anywhere] * 3,
        out_specs=pl.BlockSpec(memory_space=pltpu.VMEM),
        scratch_shapes=[
            pltpu.VMEM((STAGES, 16, 64, 512), bf16),
            pltpu.VMEM((512, 128), bf16),
            pltpu.VMEM((128, 512), bf16),
            pltpu.VMEM((2, 8, 64, 128), bf16),
            pltpu.VMEM((N_COL * 128, 256), bf16),
            pltpu.VMEM((STAGES, N_COL, 4, 16, 128), bf16),
            pltpu.VMEM((STAGES, N_COL, 4, 16, 128), bf16),
            pltpu.VMEM((2, 64, 128), f32),
            pltpu.VMEM((STAGES, 16, 512), bf16),
            pltpu.VMEM((4, 2, STAGES, 16, 512), bf16),
            pltpu.VMEM((n_blocks, 2, 2, 32, 128), f32),
            pltpu.VMEM((n_blocks, 2, 32, 128), f32),
            pltpu.VMEM((n_blocks, 2, 32, 128), f32),
            pltpu.VMEM((N_COL, 32, 128), f32),
            dma((STAGES + 2,)),
            dma((4,)),
            dma((STAGES,)),
            dma((STAGES,)),
            dma((2,)),
            dma((2,)),
            dma((n_blocks,)),
            dma((n_blocks,)),
            dma((n_blocks,)),
            dma,
        ],
        compiler_params=pltpu.CompilerParams(
            collective_id=0, has_side_effects=True, vmem_limit_bytes=60 * 1024 * 1024
        ),
    )(snapshot, basis_two, basis_three)


def solution(mesh):
    in_specs = (P("row", "col", None), P("col", None), P())
    return jax.shard_map(
        on_device, mesh=mesh, in_specs=in_specs, out_specs=P("row", "col"), check_vma=False
    )
```

time: 49.3 us -> 46 us (0.933)
  local copies, waits for them, and re-layouts: 4.43 us -> 1.38 us
    unnamed x7 -> x1, local copies, waits for them, and re-layouts: 4.43 us -> 1.38 us
where the time goes in v2:
time: 46 us; the launch traced here: 45.9 us
  Pallas kernels  44.5 us (97%)
  local copies, waits for them, and re-layouts  1.38 us (3%)
    pallas_call x1, Pallas kernels, on_device(): pl.pallas_call(kernel, out_shape=jax.ShapeDtypeStruct((64, 64), f32), in_...  44.5 us
    unnamed x1, local copies, waits for them, and re-layouts  1.38 us

profile of v2, /device:TPU:1, one launch (start us, length us, event | category | flops | bytes accessed | tf_op | source)
XLA Modules:
  0.0 45.9 jit_solution(5850978028270284965)
XLA Ops:
  0.0 44.5 %shard_map.37 = f32[64,64]{1,0:T(8,128)} custom-call(bf16[64,64,512]{2,1,0:T(8,128)(2,1)} %snap_hbm.1, bf16[64,128]{1,0:T(8,128)(2,1)} %b2_hbm.1, bf16[512,128]{1,0:T(8,128)(2,1)} %b3_hbm.1), custom_call_target="tpu_custom_call" | custom-call | tf_op jit(solution)/shard_map/pallas_call | solution.py:269
  44.5 1.4 %copy.5 = f32[64,64]{1,0:T(8,128)} copy(f32[64,64]{1,0:T(8,128)} %shard_map.37) | data formatting | bytes 32768

commit v3 on v2

--- a/solution.py
+++ b/solution.py
@@ -10,9 +10,13 @@
 
 N_COL = 16
 PLANES = 8
-STAGES = 4
+STAGES = 8
+LAG = 3
+ROWS = 64 // STAGES
+HALF = ROWS // 2
+PAIRS = HALF // 2
 OFFSETS = (0, -2, -1, 2)
-BLOCKS = ((3, 0), (3, 2), (1, 3), (2, 0), (2, 3), (0, 3), (0, 2), (0, 0))
+BLOCKS = ((0, 0), (2, 0), (0, 2), (3, 0), (0, 3), (3, 2), (2, 3), (1, 3))
 
 
 def kernel(
@@ -70,7 +74,7 @@
     load_b3 = pltpu.make_async_copy(b3_hbm, b3, load_sems.at[STAGES])
     load_b2 = pltpu.make_async_copy(b2_hbm, factor.at[core, chip], load_sems.at[STAGES + 1])
     loads = [
-        pltpu.make_async_copy(snap_hbm.at[pl.ds(16 * s, 16)], snap.at[s], load_sems.at[s])
+        pltpu.make_async_copy(snap_hbm.at[pl.ds(ROWS * s, ROWS)], snap.at[s], load_sems.at[s])
         for s in range(STAGES)
     ]
     load_b3.start()
@@ -102,9 +106,10 @@
     def first_product(s):
         loads[s].wait()
         left = b3t[...]
-        for jp in range(4):
+        for jp in range(PAIRS):
+            j = 2 * jp
             right = jnp.concatenate(
-                [snap[s, 2 * jp], snap[s, 8 + 2 * jp], snap[s, 2 * jp + 1], snap[s, 9 + 2 * jp]], axis=0
+                [snap[s, j], snap[s, HALF + j], snap[s, j + 1], snap[s, HALF + j + 1]], axis=0
             )
             inner = lax.dot_general(left, right, NT, preferred_element_type=jnp.float32)
             pair = jnp.concatenate(
@@ -131,12 +136,12 @@
     load_b2.wait()
     pl.semaphore_wait(barrier, N_COL - 1 + 3 + 4 + 3)
 
-    send_stage(0)
     own = factor.at[core, chip]
     for y in range(1, 4):
         remote(own, own, f_sems.at[0], f_sems.at[1], (row, col ^ (4 * y))).start()
     for y in range(4):
         remote(own, own, f_sems.at[0], f_sems.at[1], (z * 2 + across[0], across[1] ^ (4 * y))).start()
+    send_stage(0)
     for s in range(1, STAGES):
         first_product(s)
         send_stage(s)
@@ -159,22 +164,21 @@
         for slot, offset in enumerate(OFFSETS):
             to = plane(-offset) * 2
             if slot:
-                remote(rows.at[0, xh, s], rows.at[slot, xh, s], z_send.at[0], z_recv.at[0], (to + xh, col)).start()
-            which = 0 if slot else 1
+                remote(rows.at[0, xh, s], rows.at[slot, xh, s], z_send.at[slot], z_recv.at[slot], (to + xh, col)).start()
             remote(
                 half_out.at[s],
                 rows.at[slot, xh, s],
-                z_send.at[which],
-                z_recv.at[which],
+                z_send.at[slot],
+                z_recv.at[slot],
                 (to + across[0], across[1]),
             ).start()
 
     def second_product(s):
         stage_copy(s).wait_recv()
-        total = jnp.zeros((64, 256), jnp.float32)
+        total = jnp.zeros((8 * HALF, 256), jnp.float32)
         for c in range(0, N_COL, 2):
             left = jnp.concatenate(
-                [incoming[s, c].reshape(64, 128), incoming[s, c + 1].reshape(64, 128)], axis=1
+                [incoming[s, c].reshape(8 * HALF, 128), incoming[s, c + 1].reshape(8 * HALF, 128)], axis=1
             )
             total = total + jnp.dot(left, weights[pl.ds(c * 128, 256), :], preferred_element_type=jnp.float32)
         pacc[0] = total[:, :128]
@@ -182,7 +186,7 @@
         for r in range(4):
             halves = []
             for h in range(2):
-                every = pl.ds(4 * h + r, 8, stride=8)
+                every = pl.ds(4 * h + r, HALF, stride=8)
                 halves.append(jnp.concatenate([pacc[0, every, :], pacc[1, every, :]], axis=0))
             lanes = pl.ds(r * 128, 128)
             rows[0, xh, s, :, lanes] = jnp.where(xh == 0, halves[0], halves[1]).astype(jnp.bfloat16)
@@ -192,12 +196,9 @@
         second_product(s)
         send_rows(s)
 
-    far = rows.at[pl.ds(1, 3)]
-    near = rows.at[0, 0]
-    far_copy = remote(far, far, z_send.at[0], z_recv.at[0], here)
-    near_copy = remote(near, near, z_send.at[1], z_recv.at[1], here)
-    near_copy.wait_recv()
-    far_copy.wait_recv()
+    def slot_copy(slot):
+        piece = rows.at[slot] if slot else rows.at[0, 0]
+        return remote(piece, piece, z_send.at[slot], z_recv.at[slot], here)
 
     low = lax.broadcasted_iota(jnp.int32, (64, 128), 1) < 64
     sender = xh * 8 + chip
@@ -225,9 +226,14 @@
             def _():
                 copy.start()
 
+    arrived = set()
     for b, (slot_u, slot_v) in enumerate(BLOCKS):
-        upper = rows[slot_u, :, 0:2].reshape(64, 512)
-        lower = rows[slot_u, :, 2:4].reshape(64, 512)
+        for slot in (slot_u, slot_v):
+            if slot not in arrived:
+                slot_copy(slot).wait_recv()
+                arrived.add(slot)
+        upper = rows[slot_u, :, : STAGES // 2].reshape(64, 512)
+        lower = rows[slot_u, :, STAGES // 2 :].reshape(64, 512)
         right = rows[slot_v].reshape(128, 512)
         swapped = jnp.concatenate([rows[slot_v, 1].reshape(64, 512), rows[slot_v, 0].reshape(64, 512)], axis=0)
         m1 = lax.dot_general(upper, right, NT, preferred_element_type=jnp.float32)
@@ -235,9 +241,10 @@
         grams[b, :, 0] = jnp.where(low, m1, m2).reshape(2, 32, 128)
         grams[b, :, 1] = jnp.where(low, m2, m1).reshape(2, 32, 128)
         mate_gram(b).start()
-        if b:
-            send_gram(b - 1)
-    send_gram(len(BLOCKS) - 1)
+        if b >= LAG:
+            send_gram(b - LAG)
+    for b in range(len(BLOCKS) - LAG, len(BLOCKS)):
+        send_gram(b)
 
     pltpu.make_async_copy(parts, parts, g_recv).wait()
     total = jnp.sum(parts[...], axis=0) * (1.0 / 16384.0)
@@ -249,8 +256,8 @@
     mate_copy.wait_send()
     for s in range(STAGES):
         stage_copy(s).wait_send()
-    far_copy.wait_send()
-    near_copy.wait_send()
+    for slot in range(len(OFFSETS)):
+        slot_copy(slot).wait_send()
     for b in range(len(BLOCKS)):
         mate_gram(b).wait_send()
         for j in range(2):
@@ -268,20 +275,20 @@
     n_blocks = len(BLOCKS)
     return pl.pallas_call(
         kernel,
-        out_shape=jax.ShapeDtypeStruct((64, 64), f32),
+        out_shape=pltpu.VMEM((64, 64), f32),
         in_specs=[anywhere] * 3,
         out_specs=pl.BlockSpec(memory_space=pltpu.VMEM),
         scratch_shapes=[
-            pltpu.VMEM((STAGES, 16, 64, 512), bf16),
+            pltpu.VMEM((STAGES, ROWS, 64, 512), bf16),
             pltpu.VMEM((512, 128), bf16),
             pltpu.VMEM((128, 512), bf16),
             pltpu.VMEM((2, 8, 64, 128), bf16),
             pltpu.VMEM((N_COL * 128, 256), bf16),
-            pltpu.VMEM((STAGES, N_COL, 4, 16, 128), bf16),
-            pltpu.VMEM((STAGES, N_COL, 4, 16, 128), bf16),
-            pltpu.VMEM((2, 64, 128), f32),
-            pltpu.VMEM((STAGES, 16, 512), bf16),
-            pltpu.VMEM((4, 2, STAGES, 16, 512), bf16),
+            pltpu.VMEM((STAGES, N_COL, PAIRS, 16, 128), bf16),
+            pltpu.VMEM((STAGES, N_COL, PAIRS, 16, 128), bf16),
+            pltpu.VMEM((2, 8 * HALF, 128), f32),
+            pltpu.VMEM((STAGES, ROWS, 512), bf16),
+            pltpu.VMEM((4, 2, STAGES, ROWS, 512), bf16),
             pltpu.VMEM((n_blocks, 2, 2, 32, 128), f32),
             pltpu.VMEM((n_blocks, 2, 32, 128), f32),
             pltpu.VMEM((n_blocks, 2, 32, 128), f32),
@@ -290,8 +297,8 @@
             dma((4,)),
             dma((STAGES,)),
             dma((STAGES,)),
-            dma((2,)),
-            dma((2,)),
+            dma((4,)),
+            dma((4,)),
             dma((n_blocks,)),
             dma((n_blocks,)),
             dma((n_blocks,)),

time: 46 us -> 39.8 us (0.87); the launches traced: 45.9 us -> 39.1 us
  Pallas kernels: 44.5 us -> 38.5 us
  local copies, waits for them, and re-layouts: 1.38 us -> 0.62 us
    pallas_call x1, Pallas kernels: 44.5 us -> 38.5 us  [on_device(): pl.pallas_call(kernel, out_shape=pltpu.VMEM((64, 64), f32), in_specs=[any...]
    unnamed x1, local copies, waits for them, and re-layouts: 1.38 us -> 0.62 us
where the time goes in v3:
time: 39.8 us; the launch traced here: 39.1 us
  Pallas kernels  38.5 us (97%)
  local copies, waits for them, and re-layouts  0.62 us (2%)
    pallas_call x1, Pallas kernels, on_device(): pl.pallas_call(kernel, out_shape=pltpu.VMEM((64, 64), f32), in_specs=[any...  38.5 us

profile of v3, /device:TPU:1, one launch (start us, length us, event | category | flops | bytes accessed | tf_op | source)
XLA Modules:
  0.0 39.1 jit_solution(17183006473779160369)
XLA Ops:
  0.0 38.5 %shard_map.37 = f32[64,64]{1,0:T(8,128)S(1)} custom-call(bf16[64,64,512]{2,1,0:T(8,128)(2,1)} %snap_hbm.1, bf16[64,128]{1,0:T(8,128)(2,1)} %b2_hbm.1, bf16[512,128]{1,0:T(8,128)(2,1)} %b3_hbm.1), custom_call_target="tpu_custom_call" | custom-call | tf_op jit(solution)/shard_map/pallas_call | solution.py:276
  38.5 0.6 %copy.5 = f32[64,64]{1,0:T(8,128)} copy(f32[64,64]{1,0:T(8,128)S(1)} %shard_map.37) | data formatting | bytes 32768

commit v4 on v3

--- a/solution.py
+++ b/solution.py
@@ -11,12 +11,13 @@
 N_COL = 16
 PLANES = 8
 STAGES = 8
-LAG = 3
+BEHIND = 2
+GROUPS = ((0,), (1, 2), (3, 4), (5, 6), (7,))
 ROWS = 64 // STAGES
 HALF = ROWS // 2
 PAIRS = HALF // 2
 OFFSETS = (0, -2, -1, 2)
-BLOCKS = ((0, 0), (2, 0), (0, 2), (3, 0), (0, 3), (3, 2), (2, 3), (1, 3))
+BLOCKS = ((0, 0), (0, 2), (2, 0), (1, 3), (3, 2), (2, 3), (0, 1), (0, 3))
 
 
 def kernel(
@@ -55,10 +56,13 @@
     xh = lax.rem(row, 2)
     core = lax.rem(col, 2)
     chip = col // 2
+    x_lo = lax.rem(chip, 2)
     across = (1 - xh, col ^ 2)
 
-    def plane(offset):
-        return lax.rem(z + offset + PLANES, PLANES)
+    sign = 1 - 2 * xh
+
+    def plane(offset, away=1):
+        return lax.rem(z + away * sign * offset + PLANES, PLANES)
 
     def remote(src, dst, send_sem, recv_sem, device):
         return pltpu.make_async_remote_copy(
@@ -72,7 +76,7 @@
 
     here = (row, col)
     load_b3 = pltpu.make_async_copy(b3_hbm, b3, load_sems.at[STAGES])
-    load_b2 = pltpu.make_async_copy(b2_hbm, factor.at[core, chip], load_sems.at[STAGES + 1])
+    load_b2 = pltpu.make_async_copy(b2_hbm, factor.at[core, x_lo, chip // 2], load_sems.at[STAGES + 1])
     loads = [
         pltpu.make_async_copy(snap_hbm.at[pl.ds(ROWS * s, ROWS)], snap.at[s], load_sems.at[s])
         for s in range(STAGES)
@@ -97,8 +101,6 @@
         greet((plane(offset) * 2 + xh, col))
     for offset in OFFSETS:
         greet((plane(offset) * 2 + across[0], across[1]))
-    for y in range(1, 4):
-        greet((z * 2 + across[0], across[1] ^ (4 * y)))
 
     load_b3.wait()
     b3t[...] = b3[...].T
@@ -134,21 +136,24 @@
 
     first_product(0)
     load_b2.wait()
-    pl.semaphore_wait(barrier, N_COL - 1 + 3 + 4 + 3)
-
-    own = factor.at[core, chip]
+    pl.semaphore_wait(barrier, N_COL - 1 + 3 + 4)
+
+    own = factor.at[core, x_lo, chip // 2]
     for y in range(1, 4):
         remote(own, own, f_sems.at[0], f_sems.at[1], (row, col ^ (4 * y))).start()
-    for y in range(4):
-        remote(own, own, f_sems.at[0], f_sems.at[1], (z * 2 + across[0], across[1] ^ (4 * y))).start()
     send_stage(0)
     for s in range(1, STAGES):
         first_product(s)
         send_stage(s)
 
-    most = factor.at[core, pl.ds(0, 7)]
+    most = factor.at[core, x_lo, pl.ds(0, 3)]
     factor_copy = remote(most, most, f_sems.at[0], f_sems.at[1], here)
     factor_copy.wait_recv()
+    line = factor.at[core, x_lo]
+    other = factor.at[core, 1 - x_lo]
+    across_copy = remote(line, line, f_sems.at[4], f_sems.at[5], (z * 2 + across[0], across[1]))
+    across_copy.start()
+    remote(other, other, f_sems.at[4], f_sems.at[5], here).wait_recv()
     mate = (row, col ^ 1)
     mine = factor.at[core]
     mate_copy = remote(mine, mine, f_sems.at[2], f_sems.at[3], mate)
@@ -156,22 +161,17 @@
     weights[...] = jnp.zeros_like(weights)
     mate_copy.wait_recv()
     for c in range(N_COL):
-        block = factor[c % 2, c // 2]
+        block = factor[c % 2, (c // 2) % 2, c // 4]
         weights[pl.ds(c * 128, 64), :128] = block
         weights[pl.ds(c * 128 + 64, 64), 128:] = block
 
     def send_rows(s):
         for slot, offset in enumerate(OFFSETS):
-            to = plane(-offset) * 2
             if slot:
-                remote(rows.at[0, xh, s], rows.at[slot, xh, s], z_send.at[slot], z_recv.at[slot], (to + xh, col)).start()
-            remote(
-                half_out.at[s],
-                rows.at[slot, xh, s],
-                z_send.at[slot],
-                z_recv.at[slot],
-                (to + across[0], across[1]),
-            ).start()
+                to = (plane(offset, -1) * 2 + xh, col)
+                remote(rows.at[0, xh, s], rows.at[slot, xh, s], z_send.at[slot], z_recv.at[slot], to).start()
+            to = (plane(offset) * 2 + across[0], across[1])
+            remote(half_out.at[s], rows.at[slot, xh, s], z_send.at[slot], z_recv.at[slot], to).start()
 
     def second_product(s):
         stage_copy(s).wait_recv()
@@ -183,14 +183,19 @@
             total = total + jnp.dot(left, weights[pl.ds(c * 128, 256), :], preferred_element_type=jnp.float32)
         pacc[0] = total[:, :128]
         pacc[1] = total[:, 128:]
-        for r in range(4):
-            halves = []
-            for h in range(2):
-                every = pl.ds(4 * h + r, HALF, stride=8)
-                halves.append(jnp.concatenate([pacc[0, every, :], pacc[1, every, :]], axis=0))
-            lanes = pl.ds(r * 128, 128)
-            rows[0, xh, s, :, lanes] = jnp.where(xh == 0, halves[0], halves[1]).astype(jnp.bfloat16)
-            half_out[s, :, lanes] = jnp.where(xh == 0, halves[1], halves[0]).astype(jnp.bfloat16)
+        halves = []
+        for h in range(2):
+            tiles = []
+            for r in range(4 * h, 4 * h + 4):
+                every = pl.ds(r, HALF, stride=8)
+                tiles.append(jnp.concatenate([pacc[0, every, :], pacc[1, every, :]], axis=0))
+            halves.append(
+                jnp.concatenate(
+                    [jnp.concatenate(tiles[:2], axis=1), jnp.concatenate(tiles[2:], axis=1)], axis=0
+                )
+            )
+        rows[0, xh, s] = jnp.where(xh == 0, halves[0], halves[1]).astype(jnp.bfloat16)
+        half_out[s] = jnp.where(xh == 0, halves[1], halves[0]).astype(jnp.bfloat16)
 
     for s in range(STAGES):
         second_product(s)
@@ -226,25 +231,42 @@
             def _():
                 copy.start()
 
-    arrived = set()
-    for b, (slot_u, slot_v) in enumerate(BLOCKS):
-        for slot in (slot_u, slot_v):
-            if slot not in arrived:
-                slot_copy(slot).wait_recv()
-                arrived.add(slot)
-        upper = rows[slot_u, :, : STAGES // 2].reshape(64, 512)
-        lower = rows[slot_u, :, STAGES // 2 :].reshape(64, 512)
-        right = rows[slot_v].reshape(128, 512)
-        swapped = jnp.concatenate([rows[slot_v, 1].reshape(64, 512), rows[slot_v, 0].reshape(64, 512)], axis=0)
+    operands = {}
+
+    def operand(slot):
+        if slot not in operands:
+            slot_copy(slot).wait_recv()
+            whole = rows[slot].reshape(2, STAGES, 2, ROWS, 256)
+            flat = jnp.concatenate([whole[:, :, 0].reshape(128, 256), whole[:, :, 1].reshape(128, 256)], axis=1)
+            quarters = [flat[32 * i : 32 * i + 32] for i in range(4)]
+            operands[slot] = (
+                jnp.concatenate([quarters[0], quarters[2]], axis=0),
+                jnp.concatenate([quarters[1], quarters[3]], axis=0),
+                flat,
+                jnp.concatenate([flat[64:], flat[:64]], axis=0),
+            )
+        return operands[slot]
+
+    def gram_block(b):
+        upper, lower, _, _ = operand(BLOCKS[b][0])
+        _, _, right, swapped = operand(BLOCKS[b][1])
         m1 = lax.dot_general(upper, right, NT, preferred_element_type=jnp.float32)
         m2 = lax.dot_general(lower, swapped, NT, preferred_element_type=jnp.float32)
         grams[b, :, 0] = jnp.where(low, m1, m2).reshape(2, 32, 128)
         grams[b, :, 1] = jnp.where(low, m2, m1).reshape(2, 32, 128)
-        mate_gram(b).start()
-        if b >= LAG:
-            send_gram(b - LAG)
-    for b in range(len(BLOCKS) - LAG, len(BLOCKS)):
-        send_gram(b)
+
+    sent = 0
+    for group in GROUPS:
+        for b in group:
+            gram_block(b)
+        for b in group:
+            mate_gram(b).start()
+        while sent < group[0] - BEHIND:
+            send_gram(sent)
+            sent += 1
+    while sent < len(BLOCKS):
+        send_gram(sent)
+        sent += 1
 
     pltpu.make_async_copy(parts, parts, g_recv).wait()
     total = jnp.sum(parts[...], axis=0) * (1.0 / 16384.0)
@@ -253,6 +275,7 @@
     out_ref[32:64, :] = jnp.where(core == 0, second, first)
 
     factor_copy.wait_send()
+    across_copy.wait_send()
     mate_copy.wait_send()
     for s in range(STAGES):
         stage_copy(s).wait_send()
@@ -282,19 +305,19 @@
             pltpu.VMEM((STAGES, ROWS, 64, 512), bf16),
             pltpu.VMEM((512, 128), bf16),
             pltpu.VMEM((128, 512), bf16),
-            pltpu.VMEM((2, 8, 64, 128), bf16),
+            pltpu.VMEM((2, 2, 4, 64, 128), bf16),
             pltpu.VMEM((N_COL * 128, 256), bf16),
             pltpu.VMEM((STAGES, N_COL, PAIRS, 16, 128), bf16),
             pltpu.VMEM((STAGES, N_COL, PAIRS, 16, 128), bf16),
             pltpu.VMEM((2, 8 * HALF, 128), f32),
-            pltpu.VMEM((STAGES, ROWS, 512), bf16),
-            pltpu.VMEM((4, 2, STAGES, ROWS, 512), bf16),
+            pltpu.VMEM((STAGES, 2 * ROWS, 256), bf16),
+            pltpu.VMEM((4, 2, STAGES, 2 * ROWS, 256), bf16),
             pltpu.VMEM((n_blocks, 2, 2, 32, 128), f32),
             pltpu.VMEM((n_blocks, 2, 32, 128), f32),
             pltpu.VMEM((n_blocks, 2, 32, 128), f32),
             pltpu.VMEM((N_COL, 32, 128), f32),
             dma((STAGES + 2,)),
-            dma((4,)),
+            dma((6,)),
             dma((STAGES,)),
             dma((STAGES,)),
             dma((4,)),

time: 39.8 us -> 38.5 us (0.967)
  Pallas kernels: 38.5 us -> 37.3 us
    pallas_call x1, Pallas kernels: 38.5 us -> 37.3 us  [on_device(): pl.pallas_call(kernel, out_shape=pltpu.VMEM((64, 64), f32), in_specs=[any...]
where the time goes in v4:
time: 38.5 us; the launch traced here: 37.9 us
  Pallas kernels  37.3 us (97%)
  local copies, waits for them, and re-layouts  0.62 us (2%)
    pallas_call x1, Pallas kernels, on_device(): pl.pallas_call(kernel, out_shape=pltpu.VMEM((64, 64), f32), in_specs=[any...  37.3 us

profile of v4, /device:TPU:1, one launch (start us, length us, event | category | flops | bytes accessed | tf_op | source)
XLA Modules:
  0.0 37.9 jit_solution(10823183230014629027)
XLA Ops:
  0.0 37.3 %shard_map.37 = f32[64,64]{1,0:T(8,128)S(1)} custom-call(bf16[64,64,512]{2,1,0:T(8,128)(2,1)} %snap_hbm.1, bf16[64,128]{1,0:T(8,128)(2,1)} %b2_hbm.1, bf16[512,128]{1,0:T(8,128)(2,1)} %b3_hbm.1), custom_call_target="tpu_custom_call" | custom-call | tf_op jit(solution)/shard_map/pallas_call | solution.py:299
  37.3 0.6 %copy.5 = f32[64,64]{1,0:T(8,128)} copy(f32[64,64]{1,0:T(8,128)S(1)} %shard_map.37) | data formatting | bytes 32768

commit v5 on v4

--- a/solution.py
+++ b/solution.py
@@ -12,12 +12,13 @@
 PLANES = 8
 STAGES = 8
 BEHIND = 2
+EAGER = 2
 GROUPS = ((0,), (1, 2), (3, 4), (5, 6), (7,))
 ROWS = 64 // STAGES
 HALF = ROWS // 2
 PAIRS = HALF // 2
 OFFSETS = (0, -2, -1, 2)
-BLOCKS = ((0, 0), (0, 2), (2, 0), (1, 3), (3, 2), (2, 3), (0, 1), (0, 3))
+BLOCKS = ((0, 0), (0, 2), (2, 0), (0, 1), (0, 3), (1, 3), (3, 2), (2, 3))
 
 
 def kernel(
@@ -49,6 +50,7 @@
     m_recv,
     g_send,
     g_recv,
+    ready,
 ):
     row = lax.axis_index("row")
     col = lax.axis_index("col")
@@ -97,10 +99,30 @@
         return carry
 
     lax.fori_loop(1, N_COL, greet_column, 0)
-    for offset in OFFSETS[1:]:
-        greet((plane(offset) * 2 + xh, col))
-    for offset in OFFSETS:
-        greet((plane(offset) * 2 + across[0], across[1]))
+    greet((z * 2 + across[0], across[1]))
+
+    edges = []
+    for slot, offset in enumerate(OFFSETS):
+        if slot:
+            edges.append((plane(offset, -1), plane(offset), (xh, col)))
+            edges.append((plane(offset), plane(offset), across))
+
+    def where(test):
+        return jnp.where(test, 1, 0)
+
+    greetings, answers = N_COL, 0
+    for target, source, (there, at) in edges:
+
+        @pl.when(target > z)
+        def _():
+            greet((target * 2 + there, at))
+
+        @pl.when(source > z)
+        def _():
+            greet((source * 2 + there, at))
+
+        greetings = greetings + where(target < z) + where(source < z)
+        answers = answers + where(target > z)
 
     load_b3.wait()
     b3t[...] = b3[...].T
@@ -136,7 +158,13 @@
 
     first_product(0)
     load_b2.wait()
-    pl.semaphore_wait(barrier, N_COL - 1 + 3 + 4)
+    pl.semaphore_wait(barrier, greetings)
+    for _, source, (there, at) in edges:
+
+        @pl.when(source < z)
+        def _():
+            pl.semaphore_signal(ready, inc=1, device_id=(source * 2 + there, at), device_id_type=MESH)
+
 
     own = factor.at[core, x_lo, chip // 2]
     for y in range(1, 4):
@@ -197,6 +225,10 @@
         rows[0, xh, s] = jnp.where(xh == 0, halves[0], halves[1]).astype(jnp.bfloat16)
         half_out[s] = jnp.where(xh == 0, halves[1], halves[0]).astype(jnp.bfloat16)
 
+    @pl.when(answers > 0)
+    def _():
+        pl.semaphore_wait(ready, answers)
+
     for s in range(STAGES):
         second_product(s)
         send_rows(s)
@@ -256,12 +288,12 @@
         grams[b, :, 1] = jnp.where(low, m2, m1).reshape(2, 32, 128)
 
     sent = 0
-    for group in GROUPS:
+    for turn, group in enumerate(GROUPS):
         for b in group:
             gram_block(b)
         for b in group:
             mate_gram(b).start()
-        while sent < group[0] - BEHIND:
+        while sent < (group[-1] + 1 if turn < EAGER else group[0] - BEHIND):
             send_gram(sent)
             sent += 1
     while sent < len(BLOCKS):
@@ -326,6 +358,7 @@
             dma((n_blocks,)),
             dma((n_blocks,)),
             dma,
+            pltpu.SemaphoreType.REGULAR,
         ],
         compiler_params=pltpu.CompilerParams(
             collective_id=0, has_side_effects=True, vmem_limit_bytes=60 * 1024 * 1024

time: 38.5 us -> 38 us (0.987)
  Pallas kernels: 37.3 us -> 36.6 us
    pallas_call x1, Pallas kernels: 37.3 us -> 36.6 us  [on_device(): pl.pallas_call(kernel, out_shape=pltpu.VMEM((64, 64), f32), in_specs=[any...]
where the time goes in v5:
time: 38 us; the launch traced here: 37.2 us
  Pallas kernels  36.6 us (96%)
  local copies, waits for them, and re-layouts  0.62 us (2%)
    pallas_call x1, Pallas kernels, on_device(): pl.pallas_call(kernel, out_shape=pltpu.VMEM((64, 64), f32), in_specs=[any...  36.6 us

profile of v5, /device:TPU:1, one launch (start us, length us, event | category | flops | bytes accessed | tf_op | source)
XLA Modules:
  0.0 37.2 jit_solution(17411580735582359135)
XLA Ops:
  0.0 36.6 %shard_map.37 = f32[64,64]{1,0:T(8,128)S(1)} custom-call(bf16[64,64,512]{2,1,0:T(8,128)(2,1)} %snap_hbm.1, bf16[64,128]{1,0:T(8,128)(2,1)} %b2_hbm.1, bf16[512,128]{1,0:T(8,128)(2,1)} %b3_hbm.1), custom_call_target="tpu_custom_call" | custom-call | tf_op jit(solution)/shard_map/pallas_call | solution.py:331
  36.6 0.6 %copy.5 = f32[64,64]{1,0:T(8,128)} copy(f32[64,64]{1,0:T(8,128)S(1)} %shard_map.37) | data formatting | bytes 32768

commit v6 on v5

--- a/solution.py
+++ b/solution.py
@@ -12,8 +12,9 @@
 PLANES = 8
 STAGES = 8
 BEHIND = 2
-EAGER = 2
 GROUPS = ((0,), (1, 2), (3, 4), (5, 6), (7,))
+GROUPS_UP = ((0,), (4,), (1, 2), (3, 5), (6, 7))
+GROUPS_DOWN = ((0,), (1, 2), (3,), (4, 5), (6, 7))
 ROWS = 64 // STAGES
 HALF = ROWS // 2
 PAIRS = HALF // 2
@@ -287,18 +288,37 @@
         grams[b, :, 0] = jnp.where(low, m1, m2).reshape(2, 32, 128)
         grams[b, :, 1] = jnp.where(low, m2, m1).reshape(2, 32, 128)
 
-    sent = 0
-    for turn, group in enumerate(GROUPS):
-        for b in group:
-            gram_block(b)
-        for b in group:
-            mate_gram(b).start()
-        while sent < (group[-1] + 1 if turn < EAGER else group[0] - BEHIND):
-            send_gram(sent)
-            sent += 1
-    while sent < len(BLOCKS):
-        send_gram(sent)
-        sent += 1
+    def work_through(groups, eager):
+        operands.clear()
+        order = [b for group in groups for b in group]
+        sent = begun = 0
+        for turn, group in enumerate(groups):
+            for b in group:
+                gram_block(b)
+            for b in group:
+                mate_gram(b).start()
+            ready_to_send = begun + len(group) if turn < eager else begun - BEHIND
+            begun += len(group)
+            while sent < ready_to_send:
+                send_gram(order[sent])
+                sent += 1
+        for b in order[sent:]:
+            send_gram(b)
+
+    first_up = jnp.logical_and(z == 0, xh == 0)
+    first_down = jnp.logical_and(z == 0, xh == 1)
+
+    @pl.when(first_up)
+    def _():
+        work_through(GROUPS_UP, 2)
+
+    @pl.when(first_down)
+    def _():
+        work_through(GROUPS_DOWN, 3)
+
+    @pl.when(z > 0)
+    def _():
+        work_through(GROUPS, 2)
 
     pltpu.make_async_copy(parts, parts, g_recv).wait()
     total = jnp.sum(parts[...], axis=0) * (1.0 / 16384.0)

time: 38 us -> 37.4 us (0.984)
  the two profiles are of different devices: /device:TPU:1 before, /device:TPU:57 now
where the time goes in v6:
time: 37.4 us; the launch traced here: 37.3 us
  Pallas kernels  36.7 us (98%)
  local copies, waits for them, and re-layouts  0.62 us (2%)
    pallas_call x1, Pallas kernels, on_device(): pl.pallas_call(kernel, out_shape=pltpu.VMEM((64, 64), f32), in_specs=[any...  36.7 us

profile of v6, /device:TPU:57, one launch (start us, length us, event | category | flops | bytes accessed | tf_op | source)
XLA Modules:
  0.0 37.3 jit_solution(13538565706834420203)
XLA Ops:
  0.0 36.7 %shard_map.37 = f32[64,64]{1,0:T(8,128)S(1)} custom-call(bf16[64,64,512]{2,1,0:T(8,128)(2,1)} %snap_hbm.1, bf16[64,128]{1,0:T(8,128)(2,1)} %b2_hbm.1, bf16[512,128]{1,0:T(8,128)(2,1)} %b3_hbm.1), custom_call_target="tpu_custom_call" | custom-call | tf_op jit(solution)/shard_map/pallas_call | solution.py:351
  36.7 0.6 %copy.5 = f32[64,64]{1,0:T(8,128)} copy(f32[64,64]{1,0:T(8,128)S(1)} %shard_map.37) | data formatting | bytes 32768

commit v7 on v6

--- a/solution.py
+++ b/solution.py
@@ -13,6 +13,7 @@
 STAGES = 8
 BEHIND = 2
 GROUPS = ((0,), (1, 2), (3, 4), (5, 6), (7,))
+GROUPS_NEXT = ((0,), (1, 2), (4,), (6, 7), (3, 5))
 GROUPS_UP = ((0,), (4,), (1, 2), (3, 5), (6, 7))
 GROUPS_DOWN = ((0,), (1, 2), (3,), (4, 5), (6, 7))
 ROWS = 64 // STAGES
@@ -306,7 +307,8 @@
             send_gram(b)
 
     first_up = jnp.logical_and(z == 0, xh == 0)
-    first_down = jnp.logical_and(z == 0, xh == 1)
+    next_up = jnp.logical_and(z == 1, xh == 0)
+    first_down = jnp.logical_and(z < 2, xh == 1)
 
     @pl.when(first_up)
     def _():
@@ -316,7 +318,11 @@
     def _():
         work_through(GROUPS_DOWN, 3)
 
-    @pl.when(z > 0)
+    @pl.when(next_up)
+    def _():
+        work_through(GROUPS_NEXT, 4)
+
+    @pl.when(z > 1)
     def _():
         work_through(GROUPS, 2)
 

time: 37.4 us -> 37.4 us (level)
  no operation moved by 1% of the time
where the time goes in v7:
time: 37.4 us; the launch traced here: 37.3 us
  Pallas kernels  36.7 us (98%)
  local copies, waits for them, and re-layouts  0.62 us (2%)
    pallas_call x1, Pallas kernels, on_device(): pl.pallas_call(kernel, out_shape=pltpu.VMEM((64, 64), f32), in_specs=[any...  36.7 us

profile of v7, /device:TPU:57, one launch (start us, length us, event | category | flops | bytes accessed | tf_op | source)
XLA Modules:
  0.0 37.3 jit_solution(3611930333989517043)
XLA Ops:
  0.0 36.7 %shard_map.37 = f32[64,64]{1,0:T(8,128)S(1)} custom-call(bf16[64,64,512]{2,1,0:T(8,128)(2,1)} %snap_hbm.1, bf16[64,128]{1,0:T(8,128)(2,1)} %b2_hbm.1, bf16[512,128]{1,0:T(8,128)(2,1)} %b3_hbm.1), custom_call_target="tpu_custom_call" | custom-call | tf_op jit(solution)/shard_map/pallas_call | solution.py:357
  36.7 0.6 %copy.5 = f32[64,64]{1,0:T(8,128)} copy(f32[64,64]{1,0:T(8,128)S(1)} %shard_map.37) | data formatting | bytes 32768

commit v8 on v6

--- a/solution.py
+++ b/solution.py
@@ -12,7 +12,7 @@
 PLANES = 8
 STAGES = 8
 BEHIND = 2
-GROUPS = ((0,), (1, 2), (3, 4), (5, 6), (7,))
+GROUPS = ((0,), (1, 2), (5, 3), (6, 7), (4,))
 GROUPS_UP = ((0,), (4,), (1, 2), (3, 5), (6, 7))
 GROUPS_DOWN = ((0,), (1, 2), (3,), (4, 5), (6, 7))
 ROWS = 64 // STAGES

time: 37.4 us -> 37.4 us (level)
  no operation moved by 1% of the time
where the time goes in v8:
time: 37.4 us; the launch traced here: 37.3 us
  Pallas kernels  36.7 us (98%)
  local copies, waits for them, and re-layouts  0.62 us (2%)
    pallas_call x1, Pallas kernels, on_device(): pl.pallas_call(kernel, out_shape=pltpu.VMEM((64, 64), f32), in_specs=[any...  36.7 us

profile of v8, /device:TPU:57, one launch (start us, length us, event | category | flops | bytes accessed | tf_op | source)
XLA Modules:
  0.0 37.3 jit_solution(14389344967406422876)
XLA Ops:
  0.0 36.7 %shard_map.37 = f32[64,64]{1,0:T(8,128)S(1)} custom-call(bf16[64,64,512]{2,1,0:T(8,128)(2,1)} %snap_hbm.1, bf16[64,128]{1,0:T(8,128)(2,1)} %b2_hbm.1, bf16[512,128]{1,0:T(8,128)(2,1)} %b3_hbm.1), custom_call_target="tpu_custom_call" | custom-call | tf_op jit(solution)/shard_map/pallas_call | solution.py:351
  36.7 0.6 %copy.5 = f32[64,64]{1,0:T(8,128)} copy(f32[64,64]{1,0:T(8,128)S(1)} %shard_map.37) | data formatting | bytes 32768
